TPU v7x, 32 devices: a whole 2x2x4 slice. The times are simulated.
32 devices in a mesh: gx: 4 (over y, core), gy: 8 (over z, x).
Axes of the slice: x: 2, y: 2, z: 4, core: 2. Of those that a mesh axis runs over, the one named last changes fastest.
Arguments:
- state: float32 [4, 128, 32, 1024], P(None, 'gx', 'gy'), may hold values from -8 to 8
- diffusivity: float32 [128, 32, 1024], P('gx', 'gy'), may hold values from 0.1 to 10
Outputs:
- state_next: float32 [4, 128, 32, 1024], P(None, 'gx', 'gy')
All inputs are finite; a program needn't handle non-finite values.
Results may differ from a plain program's by a relative error of at most 0.0003.
Values sent between devices are 32-bit elements; how exact they have to be, the bound alone decides.
A program may use at most 64 MiB of HBM per device.

v0:
```python
import functools

import jax
import jax.numpy as jnp
from jax import lax
from jax.experimental import pallas as pl
from jax.experimental.pallas import tpu as pltpu
from jax.sharding import PartitionSpec as P

diff_number = 4000.0
scalar_ratio = 1.4
step_size = 0.1
LANES = 128
MESH = pl.DeviceIdType.MESH


def along_z(v):
    lane = lax.broadcasted_iota(jnp.int32, v.shape, 2)
    subs = v.shape[1]
    up = pltpu.roll(v, subs - 1, 1)
    down = pltpu.roll(v, 1, 1)
    plus1 = pltpu.roll(jnp.where(lane < 1, up, v), LANES - 1, 2)
    plus2 = pltpu.roll(jnp.where(lane < 2, up, v), LANES - 2, 2)
    minus1 = pltpu.roll(jnp.where(lane >= LANES - 1, down, v), 1, 2)
    minus2 = pltpu.roll(jnp.where(lane >= LANES - 2, down, v), 2, 2)
    return (8.0 / 12.0) * (plus1 - minus1) - (1.0 / 12.0) * (plus2 - minus2)


def tendency(rows):
    n = rows[0].shape[0] - 4
    centre = [q[2 : 2 + n] for q in rows]
    out = []
    for q, mid in zip(rows, centre):
        near = q[3 : 3 + n] - q[1 : 1 + n]
        far = q[4 : 4 + n] - q[0:n]
        dy = (8.0 / 12.0) * near - (1.0 / 12.0) * far
        out.append(-(centre[1] * dy + centre[2] * along_z(mid)))
    return out, centre


def mixed_rows(rows):
    first, centre = tendency(rows)
    middle = [s + step_size * f for s, f in zip(centre, first)]
    second, _ = tendency(middle)
    n = second[0].shape[0]
    return [
        s[2 : 2 + n] + (0.5 * step_size) * (f[2 : 2 + n] + g)
        for s, f, g in zip(centre, first, second)
    ]


def kernel(
    gx,
    gy,
    chunks,
    rounds,
    state,
    kappa,
    out,
    halo,
    kside,
    coef,
    vprev,
    qacc,
    sum_m,
    sum_v,
    inv_d,
    track_b,
    track_c,
    take_s,
    take_e,
    edge,
    near_send,
    near_recv,
    far_send,
    far_recv,
    k_send,
    k_recv,
    m_send,
    m_recv,
    v_send,
    v_recv,
):
    pos = lax.axis_index("gx")
    g = lax.axis_index("gy")
    odd = lax.rem(g, 2)
    partner = g + 1 - 2 * odd
    ahead = lax.rem(g + 2 - 4 * odd + gy, gy)
    behind = lax.rem(g - 2 + 4 * odd + gy, gy)
    nx, ny = kappa.shape[0], kappa.shape[1]
    width = nx // chunks
    tile = kappa.shape[1:]

    barrier = pltpu.get_barrier_semaphore()
    for other in (partner, ahead, behind):
        pl.semaphore_signal(barrier, inc=1, device_id={"gy": other}, device_id_type=MESH)
    for j in range(1, gx):
        pl.semaphore_signal(
            barrier, inc=1, device_id={"gx": lax.rem(pos + j, gx)}, device_id_type=MESH
        )
    pl.semaphore_wait(barrier, 3 + gx - 1)

    def near(c):
        part = pl.ds(c * width, width)
        return pltpu.make_async_remote_copy(
            src_ref=state.at[:, part],
            dst_ref=halo.at[odd, :, part],
            send_sem=near_send.at[c],
            recv_sem=near_recv.at[c],
            device_id={"gy": partner},
            device_id_type=MESH,
        )

    def far(c):
        part = pl.ds(c * width, width)
        return pltpu.make_async_remote_copy(
            src_ref=halo.at[1 - odd, :, part],
            dst_ref=halo.at[odd, :, part],
            send_sem=far_send.at[c],
            recv_sem=far_recv.at[c],
            device_id={"gy": ahead},
            device_id_type=MESH,
        )

    def k_copy(to_right):
        return pltpu.make_async_remote_copy(
            src_ref=kappa.at[nx - 1 if to_right else 0],
            dst_ref=kside.at[0 if to_right else 1],
            send_sem=k_send.at[0 if to_right else 1],
            recv_sem=k_recv.at[0 if to_right else 1],
            device_id={"gx": lax.rem(pos + (1 if to_right else gx - 1), gx)},
            device_id_type=MESH,
        )

    def bit(k):
        return lax.rem(pos // (2**k), 2)

    def sums(buf, k, send, recv):
        b = bit(k)
        return pltpu.make_async_remote_copy(
            src_ref=buf.at[k, b],
            dst_ref=buf.at[k, b],
            send_sem=send.at[k],
            recv_sem=recv.at[k],
            device_id={"gx": pos + (2**k) * (1 - 2 * b)},
            device_id_type=MESH,
        )

    @pl.when(pos < gx - 1)
    def _():
        k_copy(True).start()

    @pl.when(pos > 0)
    def _():
        k_copy(False).start()

    @pl.loop(0, chunks)
    def _(c):
        near(c).start()

    zero = jnp.zeros(tile, jnp.float32)
    one = jnp.ones(tile, jnp.float32)

    @pl.when(pos > 0)
    def _():
        k_copy(True).wait_recv()

    @pl.when(pos < gx - 1)
    def _():
        k_copy(False).wait_recv()

    @pl.when(pos == 0)
    def _():
        kside[0] = zero

    @pl.when(pos == gx - 1)
    def _():
        kside[1] = zero

    scales = (0.5 * diff_number, 0.5 * diff_number * scalar_ratio)

    def matrix_row(i, k_before, k_here, k_after, carry):
        low_sum = k_before + k_here
        up_sum = k_here + k_after
        new = []
        for m, scale in enumerate(scales):
            slack, w, head_p, head_r = carry[m]
            low = scale * low_sum
            up = scale * up_sum
            excess = 1.0 + low * slack
            inv = 1.0 / (excess + up)
            ratio = up * inv
            linv = low * inv
            w = linv * w
            coef[m, 0, i] = ratio
            coef[m, 1, i] = w
            coef[m, 2, i] = inv
            coef[m, 3, i] = linv
            coef[m, 4, i] = head_p
            new.append((excess * inv, w, head_p * ratio, head_r + head_p * w))
        return tuple(new)

    carry = tuple((one, one, one, zero) for _ in scales)
    carry = matrix_row(0, kside[0], kappa[0], kappa[1], carry)
    carry = lax.fori_loop(
        1,
        nx - 1,
        lambda i, cr: matrix_row(i, kappa[i - 1], kappa[i], kappa[i + 1], cr),
        carry,
    )
    carry = matrix_row(nx - 1, kappa[nx - 2], kappa[nx - 1], kside[1], carry)
    for m in range(2):
        _, w, head_p, head_r = carry[m]
        b = bit(0)
        sum_m[0, b, m] = head_p
        sum_m[0, b, 2 + m] = head_r
        sum_m[0, b, 4 + m] = coef[m, 0, nx - 1]
        sum_m[0, b, 6 + m] = w
        track_b[0, m] = one
        track_c[0, m] = zero
        track_b[1, m] = zero
        track_c[1, m] = one
    if rounds:
        sums(sum_m, 0, m_send, m_recv).start()

    def merge_matrix(k):
        sums(sum_m, k, m_send, m_recv).wait_recv()
        b = bit(k)
        for m in range(2):
            p1, r1 = sum_m[k, 0, m], sum_m[k, 0, 2 + m]
            last1, w1 = sum_m[k, 0, 4 + m], sum_m[k, 0, 6 + m]
            p2, r2 = sum_m[k, 1, m], sum_m[k, 1, 2 + m]
            last2, w2 = sum_m[k, 1, 4 + m], sum_m[k, 1, 6 + m]
            inv = 1.0 / (1.0 - last1 * r2)
            inv_d[k, m] = inv
            end_b, end_c = w1 * inv, last1 * p2 * inv
            start_b, start_c = r2 * end_b, p2 + r2 * end_c
            if k + 1 < rounds:
                up = bit(k + 1)
                sum_m[k + 1, up, m] = p1 * start_c
                sum_m[k + 1, up, 2 + m] = r1 + p1 * start_b
                sum_m[k + 1, up, 4 + m] = last2 + w2 * end_c
                sum_m[k + 1, up, 6 + m] = w2 * end_b

            @pl.when(b == 0)
            def _():
                for side in range(2):
                    c = track_c[side, m]
                    take_s[k, side, m] = c
                    take_e[k, side, m] = zero
                    track_b[side, m] = track_b[side, m] + c * start_b
                    track_c[side, m] = c * start_c

            @pl.when(b == 1)
            def _():
                for side in range(2):
                    c = track_b[side, m]
                    take_s[k, side, m] = zero
                    take_e[k, side, m] = c
                    track_c[side, m] = track_c[side, m] + c * end_c
                    track_b[side, m] = c * end_b

        if k + 1 < rounds:
            sums(sum_m, k + 1, m_send, m_recv).start()

    near(0).wait_recv()
    far(0).start()
    for c in range(4):
        vprev[c] = zero
        qacc[c] = zero

    @pl.loop(0, chunks)
    def _(c):
        @pl.when(c + 1 < chunks)
        def _():
            near(c + 1).wait_recv()
            far(c + 1).start()

        for k in range(rounds):

            @pl.when(c == min(k, chunks - 1))
            def _():
                merge_matrix(k)

        far(c).wait_recv()

        @pl.loop(0, width)
        def _(j):
            x = c * width + j
            rows = [
                jnp.concatenate(
                    [halo[0, f, x][ny - 4 :], state[f, x], halo[1, f, x][:4]], 0
                )
                for f in range(4)
            ]
            mixed = mixed_rows(rows)
            for f in range(4):
                m = 1 if f == 3 else 0
                v = mixed[f] * coef[m, 2, x] + coef[m, 3, x] * vprev[f]
                vprev[f] = v
                out[f, x] = v
                qacc[f] = qacc[f] + coef[m, 4, x] * v

    for f in range(4):
        edge[0, f] = zero
        edge[1, f] = zero
    if rounds:
        b = bit(0)
        for f in range(4):
            sum_v[0, b, f] = qacc[f]
            sum_v[0, b, 4 + f] = vprev[f]
        sums(sum_v, 0, v_send, v_recv).start()
    for k in range(rounds):
        sums(sum_v, k, v_send, v_recv).wait_recv()
        for f in range(4):
            m = 1 if f == 3 else 0
            q1, v1 = sum_v[k, 0, f], sum_v[k, 0, 4 + f]
            q2, v2 = sum_v[k, 1, f], sum_v[k, 1, 4 + f]
            end_a = (v1 + sum_m[k, 0, 4 + m] * q2) * inv_d[k, m]
            start_a = q2 + sum_m[k, 1, 2 + m] * end_a
            if k + 1 < rounds:
                up = bit(k + 1)
                sum_v[k + 1, up, f] = q1 + sum_m[k, 0, m] * start_a
                sum_v[k + 1, up, 4 + f] = v2 + sum_m[k, 1, 6 + m] * end_a
            for side in range(2):
                edge[side, f] = (
                    edge[side, f] + take_s[k, side, m] * start_a + take_e[k, side, m] * end_a
                )
        if k + 1 < rounds:
            sums(sum_v, k + 1, v_send, v_recv).start()

    def upward(i, after):
        x = nx - 1 - i
        new = []
        for f in range(4):
            m = 1 if f == 3 else 0
            here = out[f, x] + coef[m, 1, x] * edge[0, f] + coef[m, 0, x] * after[f]
            out[f, x] = here
            new.append(here)
        return tuple(new)

    lax.fori_loop(0, nx, upward, tuple(edge[1, f] for f in range(4)))

    @pl.loop(0, chunks)
    def _(c):
        near(c).wait_send()
        far(c).wait_send()

    @pl.when(pos < gx - 1)
    def _():
        k_copy(True).wait_send()

    @pl.when(pos > 0)
    def _():
        k_copy(False).wait_send()

    for k in range(rounds):
        sums(sum_m, k, m_send, m_recv).wait_send()
        sums(sum_v, k, v_send, v_recv).wait_send()


def body(gx, gy, state, diffusivity):
    fields, nx, ny, nz = state.shape
    subs = nz // LANES
    tile = (ny, subs, LANES)
    rounds = gx.bit_length() - 1
    assert gx == 2**rounds and gy % 2 == 0 and ny >= 4
    chunks = 8 if nx % 8 == 0 else 1
    steps = max(rounds, 1)
    f32 = jnp.float32
    dma = pltpu.SemaphoreType.DMA
    call = pl.pallas_call(
        functools.partial(kernel, gx, gy, chunks, rounds),
        out_shape=jax.ShapeDtypeStruct((fields, nx) + tile, f32),
        in_specs=[pl.BlockSpec(memory_space=pltpu.VMEM)] * 2,
        out_specs=pl.BlockSpec(memory_space=pltpu.VMEM),
        scratch_shapes=[
            pltpu.VMEM((2, fields, nx) + tile, f32),
            pltpu.VMEM((2,) + tile, f32),
            pltpu.VMEM((2, 5, nx) + tile, f32),
            pltpu.VMEM((fields,) + tile, f32),
            pltpu.VMEM((fields,) + tile, f32),
            pltpu.VMEM((steps, 2, 8) + tile, f32),
            pltpu.VMEM((steps, 2, 8) + tile, f32),
            pltpu.VMEM((steps, 2) + tile, f32),
            pltpu.VMEM((2, 2) + tile, f32),
            pltpu.VMEM((2, 2) + tile, f32),
            pltpu.VMEM((steps, 2, 2) + tile, f32),
            pltpu.VMEM((steps, 2, 2) + tile, f32),
            pltpu.VMEM((2, fields) + tile, f32),
            dma((chunks,)),
            dma((chunks,)),
            dma((chunks,)),
            dma((chunks,)),
            dma((2,)),
            dma((2,)),
            dma((steps,)),
            dma((steps,)),
            dma((steps,)),
            dma((steps,)),
        ],
        compiler_params=pltpu.CompilerParams(
            collective_id=0, has_side_effects=True, vmem_limit_bytes=40 * 2**20
        ),
        cost_estimate=pl.CostEstimate(
            flops=100 * state.size, bytes_accessed=8 * state.size, transcendentals=0
        ),
    )
    result = call(state.reshape((fields, nx) + tile), diffusivity.reshape((nx,) + tile))
    return result.reshape(state.shape)


def solution(mesh):
    return jax.shard_map(
        functools.partial(body, mesh.shape["gx"], mesh.shape["gy"]),
        mesh=mesh,
        in_specs=(P(None, "gx", "gy", None), P("gx", "gy", None)),
        out_specs=P(None, "gx", "gy", None),
        check_vma=False,
    )
```

profile of v0, /device:TPU:0, one launch (start us, length us, event | category | flops | bytes accessed | tf_op | source)
XLA Modules:
  0.0 74.1 jit_solution(16528390763547823895)
XLA Ops:
  0.0 1.3 %reshape.10.kappa = f32[32,4,8,128]{3,2,1,0:T(8,128)S(1)} reshape(f32[32,4,1024]{2,1,0:T(4,128)} %param.3) | data formatting | bytes 1048576 | tf_op jit(solution)/shard_map/reshape | solution.py:409
  1.3 3.1 %reshape.9.state = f32[4,32,4,8,128]{4,3,2,1,0:T(8,128)} reshape(f32[4,32,4,1024]{3,2,1,0:T(4,128)} %param.2) | data formatting | bytes 4194304 | tf_op jit(solution)/shard_map/reshape | solution.py:409
  4.3 0.0 copy-start
  4.3 1.6 %copy-done = f32[4,32,4,8,128]{4,3,2,1,0:T(8,128)S(1)} copy-done((f32[4,32,4,8,128]{4,3,2,1,0:T(8,128)S(1)}, f32[4,32,4,8,128]{4,3,2,1,0:T(8,128)}, u32[]{:S(2)}) %copy-start) | copy-done | bytes 2097176
  5.9 66.5 %shard_map.28 = f32[4,32,4,8,128]{4,3,2,1,0:T(8,128)S(1)} custom-call(f32[4,32,4,8,128]{4,3,2,1,0:T(8,128)S(1)} %copy-done, f32[32,4,8,128]{3,2,1,0:T(8,128)S(1)} %reshape.10.kappa), custom_call_target="tpu_custom_call" | custom-call | flops 52428800 | bytes 4194304 | tf_op jit(solution)/shard_map/pallas_call | solution.py:409
  72.4 1.7 %reshape.11 = f32[4,32,4,1024]{3,2,1,0:T(4,128)} reshape(f32[4,32,4,8,128]{4,3,2,1,0:T(8,128)S(1)} %shard_map.28) | data formatting | bytes 4194304 | tf_op jit(solution)/shard_map/reshape | solution.py:410
Async XLA Ops:
  4.3 1.6 %copy-start = (f32[4,32,4,8,128]{4,3,2,1,0:T(8,128)S(1)}, f32[4,32,4,8,128]{4,3,2,1,0:T(8,128)}, u32[]{:S(2)}) copy-start(f32[4,32,4,8,128]{4,3,2,1,0:T(8,128)} %reshape.9.state) | copy-start | bytes 6291460
where the time goes:
time: 74.3 us; the launch traced here: 74.1 us
  Pallas kernels  66.5 us (90%)
  local copies, waits for them, and re-layouts  7.61 us (10%)
    pallas_call x1, Pallas kernels, body(): call(state.reshape((fields, nx) + tile), diffusivity.reshape((nx,) + tile))  66.5 us
    reshape x1, local copies, waits for them, and re-layouts, body(): state.reshape((fields, nx) + tile)  3.05 us
    reshape x1, local copies, waits for them, and re-layouts, body(): return result.reshape(state.shape)  1.72 us
    unnamed x2, local copies, waits for them, and re-layouts  1.59 us

commit v1 on v0

v1 whole, which is shorter than its diff:
```python
import functools

import jax
import jax.numpy as jnp
from jax import lax
from jax.experimental import pallas as pl
from jax.experimental.pallas import tpu as pltpu
from jax.sharding import PartitionSpec as P

diff_number = 4000.0
scalar_ratio = 1.4
step_size = 0.1
LANES = 128
MESH = pl.DeviceIdType.MESH


def along_z(v):
    lane = lax.broadcasted_iota(jnp.int32, v.shape, 2)
    subs = v.shape[1]
    up = pltpu.roll(v, subs - 1, 1)
    down = pltpu.roll(v, 1, 1)
    plus1 = pltpu.roll(jnp.where(lane < 1, up, v), LANES - 1, 2)
    plus2 = pltpu.roll(jnp.where(lane < 2, up, v), LANES - 2, 2)
    minus1 = pltpu.roll(jnp.where(lane >= LANES - 1, down, v), 1, 2)
    minus2 = pltpu.roll(jnp.where(lane >= LANES - 2, down, v), 2, 2)
    return (8.0 / 12.0) * (plus1 - minus1) - (1.0 / 12.0) * (plus2 - minus2)


def along_y(q):
    n = q.shape[0] - 4
    near = q[3 : 3 + n] - q[1 : 1 + n]
    far = q[4 : 4 + n] - q[0:n]
    return (8.0 / 12.0) * near - (1.0 / 12.0) * far


def tendency(across, along, q):
    n = q.shape[0] - 4
    return -(across * along_y(q) + along * along_z(q[2 : 2 + n]))


PHASES = ((1, 2), (0,), (3,))


def kernel(
    gx,
    gy,
    ny,
    chunks,
    rounds,
    state,
    kappa,
    out,
    own,
    kap,
    halo,
    kside,
    coef,
    mid,
    vprev,
    qacc,
    sum_m,
    sum_v,
    inv_d,
    track_b,
    track_c,
    take_s,
    take_e,
    edge,
    own_sem,
    near_send,
    near_recv,
    far_send,
    far_recv,
    k_send,
    k_recv,
    m_send,
    m_recv,
    v_send,
    v_recv,
):
    pos = lax.axis_index("gx")
    g = lax.axis_index("gy")
    odd = lax.rem(g, 2)
    partner = g + 1 - 2 * odd
    ahead = lax.rem(g + 2 - 4 * odd + gy, gy)
    behind = lax.rem(g - 2 + 4 * odd + gy, gy)
    nx = kap.shape[0]
    width = nx // chunks
    tile = kap.shape[1:]
    subs = tile[0] // ny

    barrier = pltpu.get_barrier_semaphore()
    for other in (partner, ahead, behind):
        pl.semaphore_signal(barrier, inc=1, device_id={"gy": other}, device_id_type=MESH)
    for j in range(1, gx):
        pl.semaphore_signal(
            barrier, inc=1, device_id={"gx": lax.rem(pos + j, gx)}, device_id_type=MESH
        )

    def fields_of(ph):
        fields = PHASES[ph]
        return pl.ds(fields[0], len(fields))

    def own_copy(ph):
        f = fields_of(ph)
        return pltpu.make_async_copy(state.at[f], own.at[f], own_sem.at[ph])

    kap_copy = pltpu.make_async_copy(kappa, kap, own_sem.at[3])
    kap_copy.start()
    for ph in range(3):
        own_copy(ph).start()
    pl.semaphore_wait(barrier, 3 + gx - 1)

    def near(ph, c):
        f, part = fields_of(ph), pl.ds(c * width, width)
        return pltpu.make_async_remote_copy(
            src_ref=state.at[f, part],
            dst_ref=halo.at[odd, f, part],
            send_sem=near_send.at[ph, c],
            recv_sem=near_recv.at[ph, c],
            device_id={"gy": partner},
            device_id_type=MESH,
        )

    def far(ph, c):
        f, part = fields_of(ph), pl.ds(c * width, width)
        return pltpu.make_async_remote_copy(
            src_ref=halo.at[1 - odd, f, part],
            dst_ref=halo.at[odd, f, part],
            send_sem=far_send.at[ph, c],
            recv_sem=far_recv.at[ph, c],
            device_id={"gy": ahead},
            device_id_type=MESH,
        )

    def forward(ph, c):
        near(ph, c).wait_recv()
        far(ph, c).start()

    def k_copy(to_right):
        side = 0 if to_right else 1
        return pltpu.make_async_remote_copy(
            src_ref=kappa.at[nx - 1 if to_right else 0],
            dst_ref=kside.at[side],
            send_sem=k_send.at[side],
            recv_sem=k_recv.at[side],
            device_id={"gx": lax.rem(pos + (1 if to_right else gx - 1), gx)},
            device_id_type=MESH,
        )

    def bit(k):
        return lax.rem(pos // (2**k), 2)

    def m_copy(k):
        b = bit(k)
        return pltpu.make_async_remote_copy(
            src_ref=sum_m.at[k, b],
            dst_ref=sum_m.at[k, b],
            send_sem=m_send.at[k],
            recv_sem=m_recv.at[k],
            device_id={"gx": pos + (2**k) * (1 - 2 * b)},
            device_id_type=MESH,
        )

    def v_copy(ph, k):
        b = bit(k)
        part = pl.ds(0, 2 * len(PHASES[ph]))
        return pltpu.make_async_remote_copy(
            src_ref=sum_v.at[ph, k, b, part],
            dst_ref=sum_v.at[ph, k, b, part],
            send_sem=v_send.at[ph, k],
            recv_sem=v_recv.at[ph, k],
            device_id={"gx": pos + (2**k) * (1 - 2 * b)},
            device_id_type=MESH,
        )

    @pl.when(pos < gx - 1)
    def _():
        k_copy(True).start()

    @pl.when(pos > 0)
    def _():
        k_copy(False).start()

    for ph in range(3):

        @pl.loop(0, chunks)
        def _(c):
            near(ph, c).start()

    zero = jnp.zeros(tile, jnp.float32)
    one = jnp.ones(tile, jnp.float32)
    kap_copy.wait()

    @pl.when(pos > 0)
    def _():
        k_copy(True).wait_recv()

    @pl.when(pos < gx - 1)
    def _():
        k_copy(False).wait_recv()

    @pl.when(pos == 0)
    def _():
        kside[0] = zero

    @pl.when(pos == gx - 1)
    def _():
        kside[1] = zero

    scales = (0.5 * diff_number, 0.5 * diff_number * scalar_ratio)

    def matrix_row(i, k_before, k_here, k_after, carry):
        low_sum = k_before + k_here
        up_sum = k_here + k_after
        new = []
        for m, scale in enumerate(scales):
            slack, w, head_p, head_r = carry[m]
            low = scale * low_sum
            up = scale * up_sum
            excess = 1.0 + low * slack
            inv = 1.0 / (excess + up)
            ratio = up * inv
            linv = low * inv
            w = linv * w
            coef[m, 0, i] = ratio
            coef[m, 1, i] = w
            coef[m, 2, i] = inv
            coef[m, 3, i] = linv
            coef[m, 4, i] = head_p
            new.append((excess * inv, w, head_p * ratio, head_r + head_p * w))
        return tuple(new)

    carry = tuple((one, one, one, zero) for _ in scales)
    carry = matrix_row(0, kside[0], kap[0], kap[1], carry)
    carry = lax.fori_loop(
        1,
        nx - 1,
        lambda i, cr: matrix_row(i, kap[i - 1], kap[i], kap[i + 1], cr),
        carry,
    )
    carry = matrix_row(nx - 1, kap[nx - 2], kap[nx - 1], kside[1], carry)
    for m in range(2):
        _, w, head_p, head_r = carry[m]
        b = bit(0)
        sum_m[0, b, m] = head_p
        sum_m[0, b, 2 + m] = head_r
        sum_m[0, b, 4 + m] = coef[m, 0, nx - 1]
        sum_m[0, b, 6 + m] = w
        track_b[0, m] = one
        track_c[0, m] = zero
        track_b[1, m] = zero
        track_c[1, m] = one
    if rounds:
        m_copy(0).start()

    def merge_matrix(k):
        m_copy(k).wait_recv()
        b = bit(k)
        for m in range(2):
            p1, r1 = sum_m[k, 0, m], sum_m[k, 0, 2 + m]
            last1, w1 = sum_m[k, 0, 4 + m], sum_m[k, 0, 6 + m]
            p2, r2 = sum_m[k, 1, m], sum_m[k, 1, 2 + m]
            last2, w2 = sum_m[k, 1, 4 + m], sum_m[k, 1, 6 + m]
            inv = 1.0 / (1.0 - last1 * r2)
            inv_d[k, m] = inv
            end_b, end_c = w1 * inv, last1 * p2 * inv
            start_b, start_c = r2 * end_b, p2 + r2 * end_c
            if k + 1 < rounds:
                up = bit(k + 1)
                sum_m[k + 1, up, m] = p1 * start_c
                sum_m[k + 1, up, 2 + m] = r1 + p1 * start_b
                sum_m[k + 1, up, 4 + m] = last2 + w2 * end_c
                sum_m[k + 1, up, 6 + m] = w2 * end_b

            @pl.when(b == 0)
            def _():
                for side in range(2):
                    c = track_c[side, m]
                    take_s[k, side, m] = c
                    take_e[k, side, m] = zero
                    track_b[side, m] = track_b[side, m] + c * start_b
                    track_c[side, m] = c * start_c

            @pl.when(b == 1)
            def _():
                for side in range(2):
                    c = track_b[side, m]
                    take_s[k, side, m] = zero
                    take_e[k, side, m] = c
                    track_c[side, m] = track_c[side, m] + c * end_c
                    track_b[side, m] = c * end_b

        if k + 1 < rounds:
            m_copy(k + 1).start()

    def matrix_of(f):
        return 1 if f == 3 else 0

    def start_values(ph):
        b = bit(0)
        for j, f in enumerate(PHASES[ph]):
            sum_v[ph, 0, b, 2 * j] = qacc[f]
            sum_v[ph, 0, b, 2 * j + 1] = vprev[f]
        v_copy(ph, 0).start()

    def merge_values(ph, k):
        v_copy(ph, k).wait_recv()
        for j, f in enumerate(PHASES[ph]):
            m = matrix_of(f)
            q1, v1 = sum_v[ph, k, 0, 2 * j], sum_v[ph, k, 0, 2 * j + 1]
            q2, v2 = sum_v[ph, k, 1, 2 * j], sum_v[ph, k, 1, 2 * j + 1]
            end_a = (v1 + sum_m[k, 0, 4 + m] * q2) * inv_d[k, m]
            start_a = q2 + sum_m[k, 1, 2 + m] * end_a
            if k + 1 < rounds:
                up = bit(k + 1)
                sum_v[ph, k + 1, up, 2 * j] = q1 + sum_m[k, 0, m] * start_a
                sum_v[ph, k + 1, up, 2 * j + 1] = v2 + sum_m[k, 1, 6 + m] * end_a
            for side in range(2):
                edge[side, f] = (
                    edge[side, f] + take_s[k, side, m] * start_a + take_e[k, side, m] * end_a
                )
        if k + 1 < rounds:
            v_copy(ph, k + 1).start()

    def substitute(ph):
        fields = PHASES[ph]
        lefts = tuple(edge[0, f] for f in fields)

        def upward(i, after):
            x = nx - 1 - i
            new = []
            for f, left, nxt in zip(fields, lefts, after):
                m = matrix_of(f)
                here = out[f, x] + coef[m, 1, x] * left + coef[m, 0, x] * nxt
                out[f, x] = here
                new.append(here)
            return tuple(new)

        lax.fori_loop(0, nx, upward, tuple(edge[1, f] for f in fields))

    def rows_of(f, x, reach):
        def row(ref, y):
            return ref[x, pl.ds(y, subs, stride=ny), :]

        return jnp.stack(
            [row(halo.at[0, f], y) for y in range(ny - reach, ny)]
            + [row(own.at[f], y) for y in range(ny)]
            + [row(halo.at[1, f], y) for y in range(reach)]
        )

    def advect(ph, x):
        fields = PHASES[ph]
        wide = [rows_of(f, x, 4) for f in fields]
        if ph == 0:
            across, along = (q[2 : 6 + ny] for q in wide)
        else:
            across, along = rows_of(1, x, 2), rows_of(2, x, 2)
        firsts = [tendency(across, along, q) for q in wide]
        middles = [q[2 : 6 + ny] + step_size * t for q, t in zip(wide, firsts)]
        if ph == 0:
            mid_across, mid_along = (q[2 : 2 + ny] for q in middles)
            mid[0, x] = mid_across
            mid[1, x] = mid_along
        else:
            mid_across, mid_along = mid[0, x], mid[1, x]
        for f, q, t, p in zip(fields, wide, firsts, middles):
            second = tendency(mid_across, mid_along, p)
            mixed = q[4 : 4 + ny] + (0.5 * step_size) * (t[2 : 2 + ny] + second)
            for y in range(ny):
                out[f, x, pl.ds(y, subs, stride=ny), :] = mixed[y]

    def eliminate(f, begin):
        m = matrix_of(f)

        def down(j, carry):
            v, q = carry
            x = begin + j
            v = out[f, x] * coef[m, 2, x] + coef[m, 3, x] * v
            out[f, x] = v
            return v, q + coef[m, 4, x] * v

        v, q = lax.fori_loop(0, width, down, (vprev[f], qacc[f]))
        vprev[f] = v
        qacc[f] = q

    ahead_by = min(2, chunks)
    for c in range(ahead_by):
        forward(0, c)
    for f in range(4):
        vprev[f] = zero
        qacc[f] = zero
        edge[0, f] = zero
        edge[1, f] = zero

    for ph in range(3):
        own_copy(ph).wait()

        @pl.loop(0, chunks)
        def _(c):
            @pl.when(c + ahead_by < chunks)
            def _():
                forward(ph, c + ahead_by)

            if ph < 2:

                @pl.when(c + ahead_by >= chunks)
                def _():
                    forward(ph + 1, c + ahead_by - chunks)

            for k in range(rounds):
                if ph == 0:

                    @pl.when(c == min(k, chunks - 1))
                    def _():
                        merge_matrix(k)

                else:

                    @pl.when(c == min(2 * k + 2, chunks - 1))
                    def _():
                        merge_values(ph - 1, k)

            if ph > 0:

                @pl.when(c == min(2 * rounds + 2, chunks - 1))
                def _():
                    substitute(ph - 1)

            far(ph, c).wait_recv()

            @pl.loop(0, width)
            def _(j):
                advect(ph, c * width + j)

            for f in PHASES[ph]:
                eliminate(f, c * width)

        if rounds:
            start_values(ph)

    for k in range(rounds):
        merge_values(2, k)
    substitute(2)

    for ph in range(3):

        @pl.loop(0, chunks)
        def _(c):
            near(ph, c).wait_send()
            far(ph, c).wait_send()

    @pl.when(pos < gx - 1)
    def _():
        k_copy(True).wait_send()

    @pl.when(pos > 0)
    def _():
        k_copy(False).wait_send()

    for k in range(rounds):
        m_copy(k).wait_send()
        for ph in range(3):
            v_copy(ph, k).wait_send()


def flat(a):
    *lead, ny, nz = a.shape
    a = a.reshape(*lead, ny, nz // LANES, LANES)
    return jnp.swapaxes(a, -3, -2).reshape(*lead, ny * nz // LANES, LANES)


def body(gx, gy, state, diffusivity):
    fields, nx, ny, nz = state.shape
    subs = nz // LANES
    tile = (ny * subs, LANES)
    rounds = gx.bit_length() - 1
    assert gx == 2**rounds and gy % 2 == 0 and ny >= 4
    chunks = 8 if nx % 8 == 0 else 1
    steps = max(rounds, 1)
    f32 = jnp.float32
    dma = pltpu.SemaphoreType.DMA
    call = pl.pallas_call(
        functools.partial(kernel, gx, gy, ny, chunks, rounds),
        out_shape=jax.ShapeDtypeStruct((fields, nx) + tile, f32),
        in_specs=[pl.BlockSpec(memory_space=pltpu.HBM)] * 2,
        out_specs=pl.BlockSpec(memory_space=pltpu.VMEM),
        scratch_shapes=[
            pltpu.VMEM((fields, nx) + tile, f32),
            pltpu.VMEM((nx,) + tile, f32),
            pltpu.VMEM((2, fields, nx) + tile, f32),
            pltpu.VMEM((2,) + tile, f32),
            pltpu.VMEM((2, 5, nx) + tile, f32),
            pltpu.VMEM((2, nx, ny, subs, LANES), f32),
            pltpu.VMEM((fields,) + tile, f32),
            pltpu.VMEM((fields,) + tile, f32),
            pltpu.VMEM((steps, 2, 8) + tile, f32),
            pltpu.VMEM((3, steps, 2, 4) + tile, f32),
            pltpu.VMEM((steps, 2) + tile, f32),
            pltpu.VMEM((2, 2) + tile, f32),
            pltpu.VMEM((2, 2) + tile, f32),
            pltpu.VMEM((steps, 2, 2) + tile, f32),
            pltpu.VMEM((steps, 2, 2) + tile, f32),
            pltpu.VMEM((2, fields) + tile, f32),
            dma((4,)),
            dma((3, chunks)),
            dma((3, chunks)),
            dma((3, chunks)),
            dma((3, chunks)),
            dma((2,)),
            dma((2,)),
            dma((steps,)),
            dma((steps,)),
            dma((3, steps)),
            dma((3, steps)),
        ],
        compiler_params=pltpu.CompilerParams(
            collective_id=0, has_side_effects=True, vmem_limit_bytes=62 * 2**20
        ),
        cost_estimate=pl.CostEstimate(
            flops=100 * state.size, bytes_accessed=8 * state.size, transcendentals=0
        ),
    )
    result = call(flat(state), flat(diffusivity)).reshape(fields, nx, subs, ny, LANES)
    return jnp.swapaxes(result, -3, -2).reshape(state.shape)


def solution(mesh):
    return jax.shard_map(
        functools.partial(body, mesh.shape["gx"], mesh.shape["gy"]),
        mesh=mesh,
        in_specs=(P(None, "gx", "gy", None), P("gx", "gy", None)),
        out_specs=P(None, "gx", "gy", None),
        check_vma=False,
    )
```

time: 74.3 us -> 71.3 us (0.960)
  local copies, waits for them, and re-layouts: 7.61 us -> 3.08 us
  Pallas kernels: 66.5 us -> 68 us
    reshape x3 -> x0, local copies, waits for them, and re-layouts: 6.02 us -> none  [the longest x1 3.05 us: body(): state.reshape((fields, nx) + tile)]
    pallas_call x1, Pallas kernels: 66.5 us -> 68 us  [body(): call(flat(state), flat(diffusivity)).reshape(fields, nx, subs, ny, LANES)]
    unnamed x2 -> x1, local copies, waits for them, and re-layouts: 1.59 us -> 3.08 us
where the time goes in v1:
time: 71.3 us; the launch traced here: 71.1 us
  Pallas kernels  68 us (95%)
  local copies, waits for them, and re-layouts  3.08 us (4%)
    pallas_call x1, Pallas kernels, body(): call(flat(state), flat(diffusivity)).reshape(fields, nx, subs, ny, LANES)  68 us
    unnamed x1, local copies, waits for them, and re-layouts  3.08 us

profile of v1, /device:TPU:0, one launch (start us, length us, event | category | flops | bytes accessed | tf_op | source)
XLA Modules:
  0.0 71.1 jit_solution(15689922469260464314)
XLA Ops:
  0.0 68.0 %shard_map.28 = f32[4,32,32,128]{3,2,1,0:T(8,128)} custom-call(f32[4,32,32,128]{3,2,1,0:T(8,128)} %bitcast.16, f32[32,32,128]{2,1,0:T(8,128)} %bitcast.17), custom_call_target="tpu_custom_call" | custom-call | flops 52428800 | bytes 4194304 | tf_op jit(solution)/shard_map/pallas_call | solution.py:524
  68.0 3.1 %copy.7 = f32[4,32,4,1024]{3,2,1,0:T(4,128)} copy(f32[4,32,4,1024]{3,2,1,0:T(4,128)} %bitcast.15) | data formatting | bytes 4194304

commit v2 on v1

--- a/solution.py
+++ b/solution.py
@@ -14,7 +14,8 @@
 MESH = pl.DeviceIdType.MESH
 
 
-def along_z(v):
+def along_z(q):
+    v = q.reshape((-1,) + q.shape[-2:])
     lane = lax.broadcasted_iota(jnp.int32, v.shape, 2)
     subs = v.shape[1]
     up = pltpu.roll(v, subs - 1, 1)
@@ -23,7 +24,8 @@
     plus2 = pltpu.roll(jnp.where(lane < 2, up, v), LANES - 2, 2)
     minus1 = pltpu.roll(jnp.where(lane >= LANES - 1, down, v), 1, 2)
     minus2 = pltpu.roll(jnp.where(lane >= LANES - 2, down, v), 2, 2)
-    return (8.0 / 12.0) * (plus1 - minus1) - (1.0 / 12.0) * (plus2 - minus2)
+    change = (8.0 / 12.0) * (plus1 - minus1) - (1.0 / 12.0) * (plus2 - minus2)
+    return change.reshape(q.shape)
 
 
 def along_y(q):
@@ -233,12 +235,19 @@
 
     carry = tuple((one, one, one, zero) for _ in scales)
     carry = matrix_row(0, kside[0], kap[0], kap[1], carry)
-    carry = lax.fori_loop(
-        1,
-        nx - 1,
-        lambda i, cr: matrix_row(i, kap[i - 1], kap[i], kap[i + 1], cr),
-        carry,
-    )
+    ahead_by = min(2, chunks)
+    begin = 1
+    for c in range(ahead_by + 1):
+        until = (nx - 1) * (c + 1) // (ahead_by + 1)
+        carry = lax.fori_loop(
+            begin,
+            until,
+            lambda i, cr: matrix_row(i, kap[i - 1], kap[i], kap[i + 1], cr),
+            carry,
+        )
+        begin = until
+        if c < ahead_by:
+            forward(0, c)
     carry = matrix_row(nx - 1, kap[nx - 2], kap[nx - 1], kside[1], carry)
     for m in range(2):
         _, w, head_p, head_r = carry[m]
@@ -339,9 +348,9 @@
 
         lax.fori_loop(0, nx, upward, tuple(edge[1, f] for f in fields))
 
-    def rows_of(f, x, reach):
+    def rows_of(f, part, reach):
         def row(ref, y):
-            return ref[x, pl.ds(y, subs, stride=ny), :]
+            return ref[part, pl.ds(y, subs, stride=ny), :]
 
         return jnp.stack(
             [row(halo.at[0, f], y) for y in range(ny - reach, ny)]
@@ -349,26 +358,26 @@
             + [row(halo.at[1, f], y) for y in range(reach)]
         )
 
-    def advect(ph, x):
+    def advect(ph, part):
         fields = PHASES[ph]
-        wide = [rows_of(f, x, 4) for f in fields]
+        wide = [rows_of(f, part, 4) for f in fields]
         if ph == 0:
             across, along = (q[2 : 6 + ny] for q in wide)
         else:
-            across, along = rows_of(1, x, 2), rows_of(2, x, 2)
+            across, along = rows_of(1, part, 2), rows_of(2, part, 2)
         firsts = [tendency(across, along, q) for q in wide]
         middles = [q[2 : 6 + ny] + step_size * t for q, t in zip(wide, firsts)]
         if ph == 0:
             mid_across, mid_along = (q[2 : 2 + ny] for q in middles)
-            mid[0, x] = mid_across
-            mid[1, x] = mid_along
+            mid[0, :, part] = mid_across
+            mid[1, :, part] = mid_along
         else:
-            mid_across, mid_along = mid[0, x], mid[1, x]
+            mid_across, mid_along = mid[0, :, part], mid[1, :, part]
         for f, q, t, p in zip(fields, wide, firsts, middles):
             second = tendency(mid_across, mid_along, p)
             mixed = q[4 : 4 + ny] + (0.5 * step_size) * (t[2 : 2 + ny] + second)
             for y in range(ny):
-                out[f, x, pl.ds(y, subs, stride=ny), :] = mixed[y]
+                out[f, part, pl.ds(y, subs, stride=ny), :] = mixed[y]
 
     def eliminate(f, begin):
         m = matrix_of(f)
@@ -384,9 +393,6 @@
         vprev[f] = v
         qacc[f] = q
 
-    ahead_by = min(2, chunks)
-    for c in range(ahead_by):
-        forward(0, c)
     for f in range(4):
         vprev[f] = zero
         qacc[f] = zero
@@ -429,9 +435,7 @@
 
             far(ph, c).wait_recv()
 
-            @pl.loop(0, width)
-            def _(j):
-                advect(ph, c * width + j)
+            advect(ph, pl.ds(c * width, width))
 
             for f in PHASES[ph]:
                 eliminate(f, c * width)
@@ -491,7 +495,7 @@
             pltpu.VMEM((2, fields, nx) + tile, f32),
             pltpu.VMEM((2,) + tile, f32),
             pltpu.VMEM((2, 5, nx) + tile, f32),
-            pltpu.VMEM((2, nx, ny, subs, LANES), f32),
+            pltpu.VMEM((2, ny, nx, subs, LANES), f32),
             pltpu.VMEM((fields,) + tile, f32),
             pltpu.VMEM((fields,) + tile, f32),
             pltpu.VMEM((steps, 2, 8) + tile, f32),

time: 71.3 us -> 69.5 us (0.975)
  Pallas kernels: 68 us -> 66.3 us
    pallas_call x1, Pallas kernels: 68 us -> 66.3 us  [body(): call(flat(state), flat(diffusivity)).reshape(fields, nx, subs, ny, LANES)]
where the time goes in v2:
time: 69.5 us; the launch traced here: 69.4 us
  Pallas kernels  66.3 us (95%)
  local copies, waits for them, and re-layouts  3.08 us (4%)
    pallas_call x1, Pallas kernels, body(): call(flat(state), flat(diffusivity)).reshape(fields, nx, subs, ny, LANES)  66.3 us
    unnamed x1, local copies, waits for them, and re-layouts  3.08 us

profile of v2, /device:TPU:0, one launch (start us, length us, event | category | flops | bytes accessed | tf_op | source)
XLA Modules:
  0.0 69.4 jit_solution(13973795686407271660)
XLA Ops:
  0.0 66.3 %shard_map.28 = f32[4,32,32,128]{3,2,1,0:T(8,128)} custom-call(f32[4,32,32,128]{3,2,1,0:T(8,128)} %bitcast.16, f32[32,32,128]{2,1,0:T(8,128)} %bitcast.17), custom_call_target="tpu_custom_call" | custom-call | flops 52428800 | bytes 4194304 | tf_op jit(solution)/shard_map/pallas_call | solution.py:528
  66.3 3.1 %copy.7 = f32[4,32,4,1024]{3,2,1,0:T(4,128)} copy(f32[4,32,4,1024]{3,2,1,0:T(4,128)} %bitcast.15) | data formatting | bytes 4194304

commit v3 on v2

--- a/solution.py
+++ b/solution.py
@@ -1,4 +1,5 @@
 import functools
+import math
 
 import jax
 import jax.numpy as jnp
@@ -47,7 +48,7 @@
     gx,
     gy,
     ny,
-    chunks,
+    pieces,
     rounds,
     state,
     kappa,
@@ -87,7 +88,7 @@
     ahead = lax.rem(g + 2 - 4 * odd + gy, gy)
     behind = lax.rem(g - 2 + 4 * odd + gy, gy)
     nx = kap.shape[0]
-    width = nx // chunks
+    widths = tuple(nx // n for n in pieces)
     tile = kap.shape[1:]
     subs = tile[0] // ny
 
@@ -114,7 +115,7 @@
     pl.semaphore_wait(barrier, 3 + gx - 1)
 
     def near(ph, c):
-        f, part = fields_of(ph), pl.ds(c * width, width)
+        f, part = fields_of(ph), pl.ds(c * widths[ph], widths[ph])
         return pltpu.make_async_remote_copy(
             src_ref=state.at[f, part],
             dst_ref=halo.at[odd, f, part],
@@ -125,7 +126,7 @@
         )
 
     def far(ph, c):
-        f, part = fields_of(ph), pl.ds(c * width, width)
+        f, part = fields_of(ph), pl.ds(c * widths[ph], widths[ph])
         return pltpu.make_async_remote_copy(
             src_ref=halo.at[1 - odd, f, part],
             dst_ref=halo.at[odd, f, part],
@@ -135,9 +136,28 @@
             device_id_type=MESH,
         )
 
+    def later(ph, c, by):
+        out = []
+        start = 0
+        for p in range(ph, 3):
+            out.append((p, c + by - start, pieces[p]))
+            start += pieces[p]
+        return out
+
+    def run_later(act, ph, c, by):
+        for p, at, count in later(ph, c, by):
+
+            @pl.when((at >= 0) & (at < count))
+            def _():
+                act(p, at)
+
+    window = 4
+
     def forward(ph, c):
         near(ph, c).wait_recv()
         far(ph, c).start()
+        near(ph, c).wait_send()
+        run_later(lambda p, at: near(p, at).start(), ph, c, window)
 
     def k_copy(to_right):
         side = 0 if to_right else 1
@@ -184,11 +204,8 @@
     def _():
         k_copy(False).start()
 
-    for ph in range(3):
-
-        @pl.loop(0, chunks)
-        def _(c):
-            near(ph, c).start()
+    for c in range(window):
+        run_later(lambda p, at: near(p, at).start(), 0, c, 0)
 
     zero = jnp.zeros(tile, jnp.float32)
     one = jnp.ones(tile, jnp.float32)
@@ -235,7 +252,7 @@
 
     carry = tuple((one, one, one, zero) for _ in scales)
     carry = matrix_row(0, kside[0], kap[0], kap[1], carry)
-    ahead_by = min(2, chunks)
+    ahead_by = min(3, pieces[0])
     begin = 1
     for c in range(ahead_by + 1):
         until = (nx - 1) * (c + 1) // (ahead_by + 1)
@@ -402,22 +419,16 @@
     for ph in range(3):
         own_copy(ph).wait()
 
+        chunks, width = pieces[ph], widths[ph]
+
         @pl.loop(0, chunks)
         def _(c):
-            @pl.when(c + ahead_by < chunks)
-            def _():
-                forward(ph, c + ahead_by)
-
-            if ph < 2:
-
-                @pl.when(c + ahead_by >= chunks)
-                def _():
-                    forward(ph + 1, c + ahead_by - chunks)
+            run_later(forward, ph, c, ahead_by)
 
             for k in range(rounds):
                 if ph == 0:
 
-                    @pl.when(c == min(k, chunks - 1))
+                    @pl.when(c == min(2 * k + 1, chunks - 1))
                     def _():
                         merge_matrix(k)
 
@@ -449,9 +460,8 @@
 
     for ph in range(3):
 
-        @pl.loop(0, chunks)
+        @pl.loop(0, pieces[ph])
         def _(c):
-            near(ph, c).wait_send()
             far(ph, c).wait_send()
 
     @pl.when(pos < gx - 1)
@@ -480,12 +490,13 @@
     tile = (ny * subs, LANES)
     rounds = gx.bit_length() - 1
     assert gx == 2**rounds and gy % 2 == 0 and ny >= 4
-    chunks = 8 if nx % 8 == 0 else 1
+    pieces = tuple(math.gcd(nx, 8 * len(p)) for p in PHASES)
+    chunks = max(pieces)
     steps = max(rounds, 1)
     f32 = jnp.float32
     dma = pltpu.SemaphoreType.DMA
     call = pl.pallas_call(
-        functools.partial(kernel, gx, gy, ny, chunks, rounds),
+        functools.partial(kernel, gx, gy, ny, pieces, rounds),
         out_shape=jax.ShapeDtypeStruct((fields, nx) + tile, f32),
         in_specs=[pl.BlockSpec(memory_space=pltpu.HBM)] * 2,
         out_specs=pl.BlockSpec(memory_space=pltpu.VMEM),
@@ -519,7 +530,7 @@
             dma((3, steps)),
         ],
         compiler_params=pltpu.CompilerParams(
-            collective_id=0, has_side_effects=True, vmem_limit_bytes=62 * 2**20
+            collective_id=0, has_side_effects=True, vmem_limit_bytes=50 * 2**20
         ),
         cost_estimate=pl.CostEstimate(
             flops=100 * state.size, bytes_accessed=8 * state.size, transcendentals=0

time: 69.5 us -> 64.7 us (0.931)
  Pallas kernels: 66.3 us -> 62.2 us
  local copies, waits for them, and re-layouts: 3.08 us -> 2.36 us
    pallas_call x1, Pallas kernels: 66.3 us -> 62.2 us  [body(): call(flat(state), flat(diffusivity)).reshape(fields, nx, subs, ny, LANES)]
    unnamed x1 -> x3, local copies, waits for them, and re-layouts: 3.08 us -> 2.36 us
where the time goes in v3:
time: 64.7 us; the launch traced here: 64.6 us
  Pallas kernels  62.2 us (96%)
  local copies, waits for them, and re-layouts  2.36 us (4%)
    pallas_call x1, Pallas kernels, body(): call(flat(state), flat(diffusivity)).reshape(fields, nx, subs, ny, LANES)  62.2 us
    unnamed x3, local copies, waits for them, and re-layouts  2.36 us

profile of v3, /device:TPU:0, one launch (start us, length us, event | category | flops | bytes accessed | tf_op | source)
XLA Modules:
  0.0 64.6 jit_solution(9866297571509644562)
XLA Ops:
  0.0 0.0 copy-start
  0.0 1.0 %copy-done = f32[32,4,1024]{2,1,0:T(4,128)S(1)} copy-done((f32[32,4,1024]{2,1,0:T(4,128)S(1)}, f32[32,4,1024]{2,1,0:T(4,128)}, u32[]{:S(2)}) %copy-start) | copy-done | bytes 524312
  1.0 62.2 %shard_map.28 = f32[4,32,32,128]{3,2,1,0:T(8,128)S(1)} custom-call(f32[4,32,32,128]{3,2,1,0:T(8,128)} %bitcast.17, f32[32,32,128]{2,1,0:T(8,128)S(1)} %bitcast.16), custom_call_target="tpu_custom_call" | custom-call | flops 52428800 | bytes 4194304 | tf_op jit(solution)/shard_map/pallas_call | solution.py:539
  63.2 1.3 %copy.7 = f32[4,32,4,1024]{3,2,1,0:T(4,128)} copy(f32[4,32,4,1024]{3,2,1,0:T(4,128)S(1)} %bitcast.15) | data formatting | bytes 4194304
Async XLA Ops:
  0.0 1.0 %copy-start = (f32[32,4,1024]{2,1,0:T(4,128)S(1)}, f32[32,4,1024]{2,1,0:T(4,128)}, u32[]{:S(2)}) copy-start(f32[32,4,1024]{2,1,0:T(4,128)} %param.3) | copy-start | bytes 1572868

commit v4 on v3

--- a/solution.py
+++ b/solution.py
@@ -110,8 +110,6 @@
 
     kap_copy = pltpu.make_async_copy(kappa, kap, own_sem.at[3])
     kap_copy.start()
-    for ph in range(3):
-        own_copy(ph).start()
     pl.semaphore_wait(barrier, 3 + gx - 1)
 
     def near(ph, c):
@@ -196,16 +194,20 @@
             device_id_type=MESH,
         )
 
-    @pl.when(pos < gx - 1)
-    def _():
-        k_copy(True).start()
-
-    @pl.when(pos > 0)
-    def _():
-        k_copy(False).start()
-
     for c in range(window):
         run_later(lambda p, at: near(p, at).start(), 0, c, 0)
+
+    @pl.when(pos < gx - 1)
+    def _():
+        k_copy(True).start()
+
+    @pl.when(pos > 0)
+    def _():
+        k_copy(False).start()
+
+
+    for ph in range(3):
+        own_copy(ph).start()
 
     zero = jnp.zeros(tile, jnp.float32)
     one = jnp.ones(tile, jnp.float32)
@@ -530,13 +532,14 @@
             dma((3, steps)),
         ],
         compiler_params=pltpu.CompilerParams(
-            collective_id=0, has_side_effects=True, vmem_limit_bytes=50 * 2**20
+            collective_id=0, has_side_effects=True, vmem_limit_bytes=40 * 2**20
         ),
         cost_estimate=pl.CostEstimate(
             flops=100 * state.size, bytes_accessed=8 * state.size, transcendentals=0
         ),
     )
-    result = call(flat(state), flat(diffusivity)).reshape(fields, nx, subs, ny, LANES)
+    kap = pltpu.with_memory_space_constraint(flat(diffusivity), pltpu.HBM)
+    result = call(pltpu.with_memory_space_constraint(flat(state), pltpu.HBM), kap).reshape(fields, nx, subs, ny, LANES)
     return jnp.swapaxes(result, -3, -2).reshape(state.shape)
 
 

time: 64.7 us -> 63.7 us (0.985)
  local copies, waits for them, and re-layouts: 2.36 us -> 1.32 us
    unnamed x3 -> x1, local copies, waits for them, and re-layouts: 2.36 us -> 1.32 us
where the time goes in v4:
time: 63.7 us; the launch traced here: 63.5 us
  Pallas kernels  62.2 us (98%)
  local copies, waits for them, and re-layouts  1.32 us (2%)
    pallas_call x1, Pallas kernels, body(): call(pltpu.with_memory_space_constraint(flat(state), pltpu.HBM), kap)  62.2 us
    unnamed x1, local copies, waits for them, and re-layouts  1.32 us

profile of v4, /device:TPU:0, one launch (start us, length us, event | category | flops | bytes accessed | tf_op | source)
XLA Modules:
  0.0 63.5 jit_solution(8533050152999402224)
XLA Ops:
  0.0 62.2 %shard_map.28 = f32[4,32,32,128]{3,2,1,0:T(8,128)S(1)} custom-call(f32[4,32,32,128]{3,2,1,0:T(8,128)} %bitcast.16, f32[32,32,128]{2,1,0:T(8,128)} %bitcast.17), custom_call_target="tpu_custom_call" | custom-call | flops 52428800 | bytes 4194304 | tf_op jit(solution)/shard_map/pallas_call | solution.py:542
  62.2 1.3 %copy.7 = f32[4,32,4,1024]{3,2,1,0:T(4,128)} copy(f32[4,32,4,1024]{3,2,1,0:T(4,128)S(1)} %bitcast.15) | data formatting | bytes 4194304

commit v5 on v4

--- a/solution.py
+++ b/solution.py
@@ -149,7 +149,7 @@
             def _():
                 act(p, at)
 
-    window = 4
+    window = 6
 
     def forward(ph, c):
         near(ph, c).wait_recv()
@@ -254,7 +254,7 @@
 
     carry = tuple((one, one, one, zero) for _ in scales)
     carry = matrix_row(0, kside[0], kap[0], kap[1], carry)
-    ahead_by = min(3, pieces[0])
+    ahead_by = min(4, pieces[0])
     begin = 1
     for c in range(ahead_by + 1):
         until = (nx - 1) * (c + 1) // (ahead_by + 1)
@@ -430,7 +430,7 @@
             for k in range(rounds):
                 if ph == 0:
 
-                    @pl.when(c == min(2 * k + 1, chunks - 1))
+                    @pl.when(c == min(2 * k + 2, chunks - 1))
                     def _():
                         merge_matrix(k)
 
@@ -492,7 +492,7 @@
     tile = (ny * subs, LANES)
     rounds = gx.bit_length() - 1
     assert gx == 2**rounds and gy % 2 == 0 and ny >= 4
-    pieces = tuple(math.gcd(nx, 8 * len(p)) for p in PHASES)
+    pieces = tuple(math.gcd(nx, n) for n in (32, 8, 16))
     chunks = max(pieces)
     steps = max(rounds, 1)
     f32 = jnp.float32

time: 63.7 us -> 70.1 us (1.10)
  Pallas kernels: 62.2 us -> 68.6 us
    pallas_call x1, Pallas kernels: 62.2 us -> 68.6 us  [body(): call(pltpu.with_memory_space_constraint(flat(state), pltpu.HBM), kap)]
where the time goes in v5:
time: 70.1 us; the launch traced here: 70 us
  Pallas kernels  68.6 us (98%)
  local copies, waits for them, and re-layouts  1.32 us (2%)
    pallas_call x1, Pallas kernels, body(): call(pltpu.with_memory_space_constraint(flat(state), pltpu.HBM), kap)  68.6 us

profile of v5, /device:TPU:0, one launch (start us, length us, event | category | flops | bytes accessed | tf_op | source)
XLA Modules:
  0.0 70.0 jit_solution(12791857493011356255)
XLA Ops:
  0.0 68.6 %shard_map.28 = f32[4,32,32,128]{3,2,1,0:T(8,128)S(1)} custom-call(f32[4,32,32,128]{3,2,1,0:T(8,128)} %bitcast.16, f32[32,32,128]{2,1,0:T(8,128)} %bitcast.17), custom_call_target="tpu_custom_call" | custom-call | flops 52428800 | bytes 4194304 | tf_op jit(solution)/shard_map/pallas_call | solution.py:542
  68.7 1.3 %copy.7 = f32[4,32,4,1024]{3,2,1,0:T(4,128)} copy(f32[4,32,4,1024]{3,2,1,0:T(4,128)S(1)} %bitcast.15) | data formatting | bytes 4194304

commit v6 on v4

--- a/solution.py
+++ b/solution.py
@@ -59,6 +59,7 @@
     kside,
     coef,
     mid,
+    speeds,
     vprev,
     qacc,
     sum_m,
@@ -365,7 +366,7 @@
                 new.append(here)
             return tuple(new)
 
-        lax.fori_loop(0, nx, upward, tuple(edge[1, f] for f in fields))
+        lax.fori_loop(0, nx, upward, tuple(edge[1, f] for f in fields), unroll=4)
 
     def rows_of(f, part, reach):
         def row(ref, y):
@@ -382,8 +383,10 @@
         wide = [rows_of(f, part, 4) for f in fields]
         if ph == 0:
             across, along = (q[2 : 6 + ny] for q in wide)
+            speeds[0, :, part] = across
+            speeds[1, :, part] = along
         else:
-            across, along = rows_of(1, part, 2), rows_of(2, part, 2)
+            across, along = speeds[0, :, part], speeds[1, :, part]
         firsts = [tendency(across, along, q) for q in wide]
         middles = [q[2 : 6 + ny] + step_size * t for q, t in zip(wide, firsts)]
         if ph == 0:
@@ -408,7 +411,7 @@
             out[f, x] = v
             return v, q + coef[m, 4, x] * v
 
-        v, q = lax.fori_loop(0, width, down, (vprev[f], qacc[f]))
+        v, q = lax.fori_loop(0, width, down, (vprev[f], qacc[f]), unroll=True)
         vprev[f] = v
         qacc[f] = q
 
@@ -509,6 +512,7 @@
             pltpu.VMEM((2,) + tile, f32),
             pltpu.VMEM((2, 5, nx) + tile, f32),
             pltpu.VMEM((2, ny, nx, subs, LANES), f32),
+            pltpu.VMEM((2, ny + 4, nx, subs, LANES), f32),
             pltpu.VMEM((fields,) + tile, f32),
             pltpu.VMEM((fields,) + tile, f32),
             pltpu.VMEM((steps, 2, 8) + tile, f32),

time: 63.7 us -> 63.5 us (level)
  no operation moved by 1% of the time
where the time goes in v6:
time: 63.5 us; the launch traced here: 63.4 us
  Pallas kernels  62.1 us (98%)
  local copies, waits for them, and re-layouts  1.32 us (2%)
    pallas_call x1, Pallas kernels, body(): call(pltpu.with_memory_space_constraint(flat(state), pltpu.HBM), kap)  62.1 us
    unnamed x1, local copies, waits for them, and re-layouts  1.32 us

profile of v6, /device:TPU:0, one launch (start us, length us, event | category | flops | bytes accessed | tf_op | source)
XLA Modules:
  0.0 63.4 jit_solution(10094794925308488533)
XLA Ops:
  0.0 62.1 %shard_map.28 = f32[4,32,32,128]{3,2,1,0:T(8,128)S(1)} custom-call(f32[4,32,32,128]{3,2,1,0:T(8,128)} %bitcast.16, f32[32,32,128]{2,1,0:T(8,128)} %bitcast.17), custom_call_target="tpu_custom_call" | custom-call | flops 52428800 | bytes 4194304 | tf_op jit(solution)/shard_map/pallas_call | solution.py:546
  62.1 1.3 %copy.7 = f32[4,32,4,1024]{3,2,1,0:T(4,128)} copy(f32[4,32,4,1024]{3,2,1,0:T(4,128)S(1)} %bitcast.15) | data formatting | bytes 4194304

commit v7 on v6

--- a/solution.py
+++ b/solution.py
@@ -255,7 +255,7 @@
 
     carry = tuple((one, one, one, zero) for _ in scales)
     carry = matrix_row(0, kside[0], kap[0], kap[1], carry)
-    ahead_by = min(3, pieces[0])
+    ahead_by = min(2, pieces[0])
     begin = 1
     for c in range(ahead_by + 1):
         until = (nx - 1) * (c + 1) // (ahead_by + 1)
@@ -495,7 +495,7 @@
     tile = (ny * subs, LANES)
     rounds = gx.bit_length() - 1
     assert gx == 2**rounds and gy % 2 == 0 and ny >= 4
-    pieces = tuple(math.gcd(nx, 8 * len(p)) for p in PHASES)
+    pieces = tuple(math.gcd(nx, 8) for p in PHASES)
     chunks = max(pieces)
     steps = max(rounds, 1)
     f32 = jnp.float32

time: 63.5 us -> 66 us (1.039)
  Pallas kernels: 62.1 us -> 64.6 us
    pallas_call x1, Pallas kernels: 62.1 us -> 64.6 us  [body(): call(pltpu.with_memory_space_constraint(flat(state), pltpu.HBM), kap)]
where the time goes in v7:
time: 66 us; the launch traced here: 65.9 us
  Pallas kernels  64.6 us (98%)
  local copies, waits for them, and re-layouts  1.32 us (2%)
    pallas_call x1, Pallas kernels, body(): call(pltpu.with_memory_space_constraint(flat(state), pltpu.HBM), kap)  64.6 us
    unnamed x1, local copies, waits for them, and re-layouts  1.32 us

profile of v7, /device:TPU:0, one launch (start us, length us, event | category | flops | bytes accessed | tf_op | source)
XLA Modules:
  0.0 65.9 jit_solution(3151793864876977854)
XLA Ops:
  0.0 64.6 %shard_map.28 = f32[4,32,32,128]{3,2,1,0:T(8,128)S(1)} custom-call(f32[4,32,32,128]{3,2,1,0:T(8,128)} %bitcast.16, f32[32,32,128]{2,1,0:T(8,128)} %bitcast.17), custom_call_target="tpu_custom_call" | custom-call | flops 52428800 | bytes 4194304 | tf_op jit(solution)/shard_map/pallas_call | solution.py:546
  64.6 1.3 %copy.7 = f32[4,32,4,1024]{3,2,1,0:T(4,128)} copy(f32[4,32,4,1024]{3,2,1,0:T(4,128)S(1)} %bitcast.15) | data formatting | bytes 4194304
